TPU v7x, 512 devices: a whole 4x8x8 slice. The times are simulated.
512 devices in a mesh: expert: 64 (over x, z, core), tensor: 8 (over y).
Axes of the slice: x: 4, y: 8, z: 8, core: 2. Of those that a mesh axis runs over, the one named last changes fastest.
Arguments:
- tokens: bfloat16 [8192, 2048], P('expert', 'tensor'), may hold values from -6 to 6
- cotangent: bfloat16 [8192, 2048], P('expert', 'tensor'), may hold values from -6 to 6
- route_ids: int32 [8192, 6], P('expert'), may hold values from 0 to 63, all different within a row
- route_weights: float32 [8192, 6], P('expert'), may hold values from 0.05 to 0.5
- shared_gate: bfloat16 [1408, 2048], P('tensor'), may hold values from -0.125 to 0.125
- shared_up: bfloat16 [1408, 2048], P('tensor'), may hold values from -0.125 to 0.125
- shared_down: bfloat16 [1408, 2048], P('tensor'), may hold values from -0.15625 to 0.15625
- expert_gate: bfloat16 [64, 1408, 2048], P('expert', 'tensor'), may hold values from -0.125 to 0.125
- expert_up: bfloat16 [64, 1408, 2048], P('expert', 'tensor'), may hold values from -0.125 to 0.125
- expert_down: bfloat16 [64, 1408, 2048], P('expert', 'tensor'), may hold values from -0.15625 to 0.15625
Outputs:
- layer_output: bfloat16 [8192, 2048], P('expert', 'tensor')
- input_grad: bfloat16 [8192, 2048], P('expert', 'tensor')
Inputs may be any that keep to these rules, and one draw needn't show every extreme that they name: `route_ids`: each row names 6 different experts.
All inputs are finite; a program needn't handle non-finite values.
Results may differ from a plain program's by a relative error of at most 0.0051.
Values may be sent and summed in bfloat16 or wider, within the bound.
A program may use at most 64 MiB of HBM per device.

v0:
```python
import jax
import jax.numpy as jnp
from jax import lax
from jax.sharding import PartitionSpec as P


def silu_parts(pre_act):
    sigmoid_value = jax.nn.sigmoid(pre_act)
    return (pre_act * sigmoid_value, sigmoid_value * (1.0 + pre_act * (1.0 - sigmoid_value)))


def on_device(
    tokens,
    cotangent,
    route_ids,
    route_weights,
    shared_gate,
    shared_up,
    shared_down,
    expert_gate,
    expert_up,
    expert_down,
):
    expert_count = lax.axis_size("expert")
    tok_rows, top_count = route_ids.shape
    local_experts = expert_gate.shape[0]
    all_experts = local_experts * expert_count
    capacity = tok_rows * top_count // (2 * all_experts)
    slot_total = all_experts * capacity
    flat_ids = route_ids.reshape(-1)
    one_hot = (flat_ids[:, None] == jnp.arange(all_experts, dtype=jnp.int32)[None, :]).astype(
        jnp.int32
    )
    rank_in = jnp.sum((jnp.cumsum(one_hot, axis=0) - one_hot) * one_hot, axis=1)
    kept_mask = rank_in < capacity
    slot_index = jnp.where(kept_mask, flat_ids * capacity + rank_in, slot_total)
    slot_match = jnp.arange(slot_total, dtype=jnp.int32)[:, None] == slot_index[None, :]
    dispatch = jnp.any(slot_match.reshape(slot_total, tok_rows, top_count), axis=2).astype(
        jnp.bfloat16
    )
    gate_flat = route_weights.reshape(-1)
    slot_gate = jnp.sum(jnp.where(slot_match, gate_flat[None, :], 0.0), axis=1)
    gate_dispatch = dispatch.astype(jnp.float32) * slot_gate[:, None]
    x_full, c_full = (
        lax.all_gather(tokens, "tensor", axis=1, tiled=True),
        lax.all_gather(cotangent, "tensor", axis=1, tiled=True),
    )
    x_slots = jnp.dot(dispatch, x_full, preferred_element_type=jnp.float32).astype(jnp.bfloat16)
    g_slots = (
        slot_gate[:, None] * jnp.dot(dispatch, c_full, preferred_element_type=jnp.float32)
    ).astype(jnp.bfloat16)
    x_recv, g_recv = (
        lax.all_to_all(x_slots, "expert", split_axis=0, concat_axis=0, tiled=True),
        lax.all_to_all(g_slots, "expert", split_axis=0, concat_axis=0, tiled=True),
    )

    def owner_layout(values):
        shaped = values.reshape(expert_count, local_experts, capacity, values.shape[-1])
        return shaped.transpose(1, 0, 2, 3).reshape(
            local_experts, expert_count * capacity, values.shape[-1]
        )

    def source_layout(values):
        shaped = values.reshape(local_experts, expert_count, capacity, values.shape[-1])
        return shaped.transpose(1, 0, 2, 3).reshape(slot_total, values.shape[-1])

    x_own = owner_layout(x_recv)
    g_own = owner_layout(g_recv)
    gate_pre = jnp.einsum("erd,efd->erf", x_own, expert_gate, preferred_element_type=jnp.float32)
    up_pre = jnp.einsum("erd,efd->erf", x_own, expert_up, preferred_element_type=jnp.float32)
    act_value, act_slope = silu_parts(gate_pre)
    hidden = (act_value * up_pre).astype(jnp.bfloat16)
    grad_hidden = jnp.einsum("erd,efd->erf", g_own, expert_down, preferred_element_type=jnp.float32)
    grad_gate = (grad_hidden * up_pre * act_slope).astype(jnp.bfloat16)
    grad_up = (grad_hidden * act_value).astype(jnp.bfloat16)
    value_part = source_layout(
        jnp.einsum("erf,efd->erd", hidden, expert_down, preferred_element_type=jnp.float32).astype(
            jnp.bfloat16
        )
    )
    grads_joined = jnp.concatenate((grad_gate, grad_up), axis=2)
    weights_joined = jnp.concatenate((expert_gate, expert_up), axis=1)
    input_term = jnp.einsum(
        "erf,efd->erd", grads_joined, weights_joined, preferred_element_type=jnp.float32
    )
    input_part = source_layout(input_term.astype(jnp.bfloat16))
    shared_gate_pre = jnp.einsum(
        "td,fd->tf", x_full, shared_gate, preferred_element_type=jnp.float32
    )
    shared_up_pre = jnp.einsum("td,fd->tf", x_full, shared_up, preferred_element_type=jnp.float32)
    shared_act, shared_slope = silu_parts(shared_gate_pre)
    shared_hidden = (shared_act * shared_up_pre).astype(jnp.bfloat16)
    shared_value = jnp.dot(shared_hidden, shared_down, preferred_element_type=jnp.float32)
    shared_grad_hidden = jnp.einsum(
        "td,fd->tf", c_full, shared_down, preferred_element_type=jnp.float32
    )
    shared_grad_gate = (shared_grad_hidden * shared_up_pre * shared_slope).astype(jnp.bfloat16)
    shared_grad_up = (shared_grad_hidden * shared_act).astype(jnp.bfloat16)
    shared_input = jnp.dot(shared_grad_gate, shared_gate, preferred_element_type=jnp.float32)
    shared_input = shared_input + jnp.dot(
        shared_grad_up, shared_up, preferred_element_type=jnp.float32
    )
    value_back, input_back = (
        lax.all_to_all(value_part, "expert", split_axis=0, concat_axis=0, tiled=True),
        lax.all_to_all(input_part, "expert", split_axis=0, concat_axis=0, tiled=True),
    )
    early_value = shared_value + jnp.einsum(
        "st,sd->td",
        gate_dispatch,
        value_back.astype(jnp.float32),
        precision=lax.Precision.HIGHEST,
        preferred_element_type=jnp.float32,
    )
    early_input = shared_input + jnp.einsum(
        "st,sd->td",
        dispatch,
        input_back,
        precision=lax.Precision.HIGHEST,
        preferred_element_type=jnp.float32,
    )
    value_total, input_total = (
        lax.psum_scatter(early_value, "tensor", scatter_dimension=1, tiled=True),
        lax.psum_scatter(early_input, "tensor", scatter_dimension=1, tiled=True),
    )
    return (value_total.astype(jnp.bfloat16), input_total.astype(jnp.bfloat16))


def solution(mesh):
    in_specs = (
        P("expert", "tensor"),
        P("expert", "tensor"),
        P("expert", None),
        P("expert", None),
        P("tensor", None),
        P("tensor", None),
        P("tensor", None),
        P("expert", "tensor", None),
        P("expert", "tensor", None),
        P("expert", "tensor", None),
    )
    out_specs = (P("expert", "tensor"), P("expert", "tensor"))
    return jax.shard_map(
        on_device, mesh=mesh, in_specs=in_specs, out_specs=out_specs, check_vma=False
    )
```

profile of v0, /device:TPU:2, one launch (start us, length us, event | category | flops | bytes accessed | tf_op | source)
XLA Modules:
  0.0 333.4 jit_solution(1822526318146382311)
XLA Ops:
  7.2 0.8 broadcast_multiply_fusion
  7.9 0.8 copy.19
  9.0 27.1 %all_gather.6 = bf16[128,2048]{1,0:T(8,128)(2,1)S(1)} all-gather(bf16[128,256]{1,0:T(8,128)(2,1)} %param.10), channel_id=1, replica_groups=mesh['expert'=64,'tensor'=8] {'tensor'}, dimensions={1}, use_global_device_ids=true | all-gather | bytes 589824 | tf_op jit(solution)/shard_map/all_gather | solution.py:45
  36.3 1.8 reduce-window.6
  38.1 0.3 slice_reduce_fusion
  38.4 0.1 fusion.15
  38.7 0.2 fusion.2
  38.9 0.6 convolution_convert_fusion.2
  39.5 1.6 all_to_all.32
  41.1 14.0 %all-to-all-start = ((bf16[64,6,2048]{2,1,0:T(8,128)(2,1)}), bf16[64,6,2048]{2,1,0:T(8,128)(2,1)S(1)}, u32[]{:S(2)}, u32[]{:S(2)}) async-start(bf16[64,6,2048]{2,1,0:T(8,128)(2,1)} %all_to_all.32), calls=%async_computation | async-start | bytes 4194304 | tf_op jit(solution)/shard_map/all_to_all | solution.py:53
  55.4 0.2 select_reduce_fusion
  55.6 25.5 %all_gather.7 = bf16[128,2048]{1,0:T(8,128)(2,1)S(1)} all-gather(bf16[128,256]{1,0:T(8,128)(2,1)S(1)} %copy-done.14), channel_id=1, replica_groups=mesh['expert'=64,'tensor'=8] {'tensor'}, dimensions={1}, use_global_device_ids=true | all-gather | bytes 589824 | tf_op jit(solution)/shard_map/all_gather | solution.py:46
  81.1 0.8 copy-done.3
  81.9 1.7 multiply_convert_fusion
  83.6 3.7 %all_to_all.38 = bf16[64,6,2048]{2,1,0:T(8,128)(2,1)} reshape(bf16[384,2048]{1,0:T(8,128)(2,1)} %multiply_convert_fusion) | data formatting | bytes 3145728 | tf_op jit(solution)/shard_map/all_to_all | solution.py:54
  87.3 17.3 %all-to-all-done = bf16[64,6,2048]{2,1,0:T(8,128)(2,1)S(1)} async-done(((bf16[64,6,2048]{2,1,0:T(8,128)(2,1)}), bf16[64,6,2048]{2,1,0:T(8,128)(2,1)S(1)}, u32[]{:S(2)}, u32[]{:S(2)}) %all-to-all-start) | async-done | bytes 1572896 | tf_op jit(solution)/shard_map/all_to_all | solution.py:53
  104.6 1.3 copy-done.2
  105.9 7.7 %all-to-all-start.2 = ((bf16[64,6,2048]{2,1,0:T(8,128)(2,1)}), bf16[64,6,2048]{2,1,0:T(8,128)(2,1)}, u32[]{:S(2)}, u32[]{:S(2)}) async-start(bf16[64,6,2048]{2,1,0:T(8,128)(2,1)} %all_to_all.38), calls=%async_computation.3 | async-start | bytes 4194304 | tf_op jit(solution)/shard_map/all_to_all | solution.py:54
  113.6 2.6 all_to_all.34
  116.3 1.8 fusion.6
  118.1 0.7 fusion.8
  118.8 0.7 copy-done.9
  119.5 0.6 convolution_convert_fusion
  120.2 1.6 all_to_all.35
  121.7 41.4 %all-to-all-done.2 = bf16[64,6,2048]{2,1,0:T(8,128)(2,1)} async-done(((bf16[64,6,2048]{2,1,0:T(8,128)(2,1)}), bf16[64,6,2048]{2,1,0:T(8,128)(2,1)}, u32[]{:S(2)}, u32[]{:S(2)}) %all-to-all-start.2) | async-done | bytes 1572896 | tf_op jit(solution)/shard_map/all_to_all | solution.py:54
  163.1 7.5 %all-to-all-start.1 = ((bf16[64,6,2048]{2,1,0:T(8,128)(2,1)}), bf16[64,6,2048]{2,1,0:T(8,128)(2,1)S(1)}, u32[]{:S(2)}, u32[]{:S(2)}) async-start(bf16[64,6,2048]{2,1,0:T(8,128)(2,1)} %all_to_all.35), calls=%async_computation.1 | async-start | bytes 4194304 | tf_op jit(solution)/shard_map/all_to_all | solution.py:104
  170.6 3.7 %all_to_all.40 = bf16[384,2048]{1,0:T(8,128)(2,1)} reshape(bf16[64,6,2048]{2,1,0:T(8,128)(2,1)} %all-to-all-done.2) | data formatting | bytes 3145728 | tf_op jit(solution)/shard_map/all_to_all | solution.py:54
  174.4 2.3 fusion.20
  176.7 2.2 convolution_convert_fusion.1
  178.9 3.7 %all_to_all.41 = bf16[64,6,2048]{2,1,0:T(8,128)(2,1)} reshape(bf16[384,2048]{1,0:T(8,128)(2,1)} %convolution_convert_fusion.1) | data formatting | bytes 3145728 | tf_op jit(solution)/shard_map/all_to_all | solution.py:105
  182.5 37.6 %all-to-all-done.1 = bf16[64,6,2048]{2,1,0:T(8,128)(2,1)S(1)} async-done(((bf16[64,6,2048]{2,1,0:T(8,128)(2,1)}), bf16[64,6,2048]{2,1,0:T(8,128)(2,1)S(1)}, u32[]{:S(2)}, u32[]{:S(2)}) %all-to-all-start.1) | async-done | bytes 1572896 | tf_op jit(solution)/shard_map/all_to_all | solution.py:104
  220.2 1.3 copy-done.1
  221.5 7.5 %all-to-all-start.3 = ((bf16[64,6,2048]{2,1,0:T(8,128)(2,1)}), bf16[64,6,2048]{2,1,0:T(8,128)(2,1)S(1)}, u32[]{:S(2)}, u32[]{:S(2)}) async-start(bf16[64,6,2048]{2,1,0:T(8,128)(2,1)} %all_to_all.41), calls=%async_computation.4 | async-start | bytes 4194304 | tf_op jit(solution)/shard_map/all_to_all | solution.py:105
  229.0 0.2 reduce-scatter.3.cloned.1.call-start
  229.3 1.5 fusion.38
  230.8 1.5 fusion.37
  232.3 1.4 fusion.25
  233.7 3.7 %all_to_all.37 = bf16[384,2048]{1,0:T(8,128)(2,1)} reshape(bf16[64,6,2048]{2,1,0:T(8,128)(2,1)} %copy-done.1) | data formatting | bytes 3145728 | tf_op jit(solution)/shard_map/all_to_all | solution.py:104
  237.4 3.9 %convolution_add_fusion.2 = f32[128,2048]{1,0:T(8,128)} fusion(f32[128,2048]{1,0:T(8,128)} %fusion.25, bf16[384,2048]{1,0:T(8,128)(2,1)} %all_to_all.37, f32[384]{0:T(512)S(1)} %select_reduce_fusion, pred[384,128]{1,0:T(8,128)(4,1)S(1)} %fusion.2), kind=kOutput, calls=%fused_computation.6 | convolution fusion | flops 1208369152 | bytes 3720704 | tf_op jit(solution)/shard_map/st,sd->td/dot_general | solution.py:107
  241.4 1.6 fusion.39
  243.0 1.2 fusion.26
  244.2 1.3 convolution_add_fusion.1
  245.6 33.0 %all-to-all-done.3 = bf16[64,6,2048]{2,1,0:T(8,128)(2,1)S(1)} async-done(((bf16[64,6,2048]{2,1,0:T(8,128)(2,1)}), bf16[64,6,2048]{2,1,0:T(8,128)(2,1)S(1)}, u32[]{:S(2)}, u32[]{:S(2)}) %all-to-all-start.3) | async-done | bytes 1572896 | tf_op jit(solution)/shard_map/all_to_all | solution.py:105
  278.5 1.4 all_to_all.43
  280.0 3.2 convolution_add_fusion
  283.2 1.5 convert_element_type.67
  284.8 40.3 %reduce-scatter.5.cloned.1.call-done = f32[128,256]{1,0:T(8,128)} async-done(((f32[128,2048]{1,0:T(8,128)}), f32[128,256]{1,0:T(8,128)}) %reduce-scatter.5.cloned.1.call-update) | async-done | bytes 131088 | tf_op jit(solution)/shard_map/reduce_scatter | solution.py:123
  325.1 1.5 convert_element_type.76
  (43 shorter events, 1.0 us)
Async XLA Ops:
  7.2 112.4 %copy-start = (bf16[1,176,2048]{2,1,0:T(8,128)(2,1)S(1)}, bf16[1,176,2048]{2,1,0:T(8,128)(2,1)}, u32[]{:S(2)}) copy-start(bf16[1,176,2048]{2,1,0:T(8,128)(2,1)} %param.19) | copy-start | bytes 2162692
  41.1 14.0 %copy-start.15 = (f32[128,6]{0,1:T(8,128)S(1)}, f32[128,6]{0,1:T(8,128)}, u32[]{:S(2)}) copy-start(f32[128,6]{0,1:T(8,128)} %param.13) | copy-start | bytes 9220
  41.1 14.5 %copy-start.14 = (bf16[128,256]{1,0:T(8,128)(2,1)S(1)}, bf16[128,256]{1,0:T(8,128)(2,1)}, u32[]{:S(2)}) copy-start(bf16[128,256]{1,0:T(8,128)(2,1)} %param.11) | copy-start | bytes 196612
  41.1 63.5 %all-to-all-start = ((bf16[64,6,2048]{2,1,0:T(8,128)(2,1)}), bf16[64,6,2048]{2,1,0:T(8,128)(2,1)S(1)}, u32[]{:S(2)}, u32[]{:S(2)}) async-start(bf16[64,6,2048]{2,1,0:T(8,128)(2,1)} %all_to_all.32), calls=%async_computation | async-start | bytes 4194304 | tf_op jit(solution)/shard_map/all_to_all | solution.py:53
  81.1 0.8 copy-start.3
  104.6 1.3 copy-start.2
  105.9 57.2 %all-to-all-start.2 = ((bf16[64,6,2048]{2,1,0:T(8,128)(2,1)}), bf16[64,6,2048]{2,1,0:T(8,128)(2,1)}, u32[]{:S(2)}, u32[]{:S(2)}) async-start(bf16[64,6,2048]{2,1,0:T(8,128)(2,1)} %all_to_all.38), calls=%async_computation.3 | async-start | bytes 4194304 | tf_op jit(solution)/shard_map/all_to_all | solution.py:54
  116.3 1.9 copy-start.12
  118.1 2.0 copy-start.8
  118.8 0.7 copy-start.9
  163.1 57.1 %all-to-all-start.1 = ((bf16[64,6,2048]{2,1,0:T(8,128)(2,1)}), bf16[64,6,2048]{2,1,0:T(8,128)(2,1)S(1)}, u32[]{:S(2)}, u32[]{:S(2)}) async-start(bf16[64,6,2048]{2,1,0:T(8,128)(2,1)} %all_to_all.35), calls=%async_computation.1 | async-start | bytes 4194304 | tf_op jit(solution)/shard_map/all_to_all | solution.py:104
  174.4 2.3 copy-start.11
  174.4 2.3 copy-start.13
  220.2 1.3 copy-start.1
  221.5 57.1 %all-to-all-start.3 = ((bf16[64,6,2048]{2,1,0:T(8,128)(2,1)}), bf16[64,6,2048]{2,1,0:T(8,128)(2,1)S(1)}, u32[]{:S(2)}, u32[]{:S(2)}) async-start(bf16[64,6,2048]{2,1,0:T(8,128)(2,1)} %all_to_all.41), calls=%async_computation.4 | async-start | bytes 4194304 | tf_op jit(solution)/shard_map/all_to_all | solution.py:105
  229.0 54.2 %reduce-scatter.3.cloned.1.call-start = ((), (), s32[]{:S(2)}) async-start(), calls=%async_computation.6 | async-start | bytes 1179648 | tf_op jit(solution)/shard_map/reduce_scatter | solution.py:122
  229.2 3.1 copy-start.5
  230.8 1.5 copy-start.10
  237.4 3.9 %copy-start.4 = (bf16[128,2048]{1,0:T(8,128)(2,1)S(1)}, bf16[128,2048]{1,0:T(8,128)(2,1)}, u32[]{:S(2)}) copy-start(bf16[128,2048]{1,0:T(8,128)(2,1)} %copy-done.3) | copy-start | bytes 1572868
  241.3 83.8 %reduce-scatter.5.cloned.1.call-start = ((), (), s32[]{:S(2)}) async-start(), calls=%async_computation.7 | async-start | bytes 1179648 | tf_op jit(solution)/shard_map/reduce_scatter | solution.py:123
  241.4 1.6 copy-start.6
  241.4 2.8 copy-start.7
Sparse Core Ops, SparseCore 0:
  241.4 40.5 reduce-scatter.2
  284.8 40.1 reduce-scatter.4
where the time goes:
time: 335 us; the launch traced here: 333 us
  waiting for transfers between devices  170 us (51%)
  blocking collectives  52.6 us (16%)
  starting transfers between devices  37 us (11%)
  local copies, waits for them, and re-layouts  28.1 us (8%)
  matrix products  25.5 us (8%)
  between operations  14.4 us (4%)
  other arithmetic  6.19 us (2%)
    all_to_all x1, waiting for transfers between devices, on_device(): lax.all_to_all(g_slots, 'expert', split_axis=0, concat_axis=0, tiled=True)  41.4 us
    reduce_scatter x1, waiting for transfers between devices, on_device(): lax.psum_scatter(early_input, 'tensor', scatter_dimension=1, tiled=True)  40.3 us
    all_to_all x1, waiting for transfers between devices, on_device(): lax.all_to_all(value_part, 'expert', split_axis=0, concat_axis=0, tiled=T...  37.6 us
    all_to_all x1, waiting for transfers between devices, on_device(): lax.all_to_all(input_part, 'expert', split_axis=0, concat_axis=0, tiled=T...  33 us
    all_gather x1, blocking collectives, on_device(): lax.all_gather(tokens, 'tensor', axis=1, tiled=True)  27.1 us
    all_gather x1, blocking collectives, on_device(): lax.all_gather(cotangent, 'tensor', axis=1, tiled=True)  25.5 us
    all_to_all x1, waiting for transfers between devices, on_device(): lax.all_to_all(x_slots, 'expert', split_axis=0, concat_axis=0, tiled=True)  17.3 us
    all_to_all x1, starting transfers between devices, on_device(): lax.all_to_all(x_slots, 'expert', split_axis=0, concat_axis=0, tiled=True)  14 us
  transfers between devices with their start and end apart: 6, of which 5 were waited for; matrix products, arithmetic and copies ran while one was open for 8% of the time, Pallas kernels for 0%

commit v1 on v0

--- a/solution.py
+++ b/solution.py
@@ -43,7 +43,9 @@
     gate_dispatch = dispatch.astype(jnp.float32) * slot_gate[:, None]
     x_full, c_full = (
         lax.all_gather(tokens, "tensor", axis=1, tiled=True),
-        lax.all_gather(cotangent, "tensor", axis=1, tiled=True),
+        jnp.concatenate(
+            lax.all_to_all(jnp.stack([cotangent] * lax.axis_size("tensor")), "tensor", 0, 0), axis=1
+        ),
     )
     x_slots = jnp.dot(dispatch, x_full, preferred_element_type=jnp.float32).astype(jnp.bfloat16)
     g_slots = (

time: 335 us -> 347 us (1.036)
  waiting for transfers between devices: 170 us -> 195 us
  blocking collectives: 52.6 us -> 31 us
  starting transfers between devices: 37 us -> 44 us
    all_gather x1 -> x0, blocking collectives: 25.5 us -> none  [on_device(): lax.all_gather(cotangent, 'tensor', axis=1, tiled=True)]
    all_to_all x1, waiting for transfers between devices: 17.3 us -> 42.6 us  [on_device(): lax.all_to_all(x_slots, 'expert', split_axis=0, concat_axis=0, tiled=True)]
    all_to_all x0 -> x1, starting transfers between devices: none -> 7.1 us  [on_device(): lax.all_to_all(jnp.stack([cotangent] * lax.axis_size('tensor')), 'tensor'...]
    all_gather x1, blocking collectives: 27.1 us -> 31 us  [on_device(): lax.all_gather(tokens, 'tensor', axis=1, tiled=True)]
  transfers between devices with their start and end apart: 6 -> 7, of which waited for: 5 -> 5; matrix products, arithmetic and copies ran while one was open for 8% -> 9% of each run, Pallas kernels for 0% -> 0%
where the time goes in v1:
time: 347 us; the launch traced here: 346 us
  waiting for transfers between devices  195 us (56%)
  starting transfers between devices  44 us (13%)
  blocking collectives  31 us (9%)
  local copies, waits for them, and re-layouts  29.4 us (8%)
  matrix products  26.5 us (8%)
  between operations  14.4 us (4%)
  other arithmetic  5.44 us (2%)
    all_to_all x1, waiting for transfers between devices, on_device(): lax.all_to_all(x_slots, 'expert', split_axis=0, concat_axis=0, tiled=True)  42.6 us
    all_to_all x1, waiting for transfers between devices, on_device(): lax.all_to_all(g_slots, 'expert', split_axis=0, concat_axis=0, tiled=True)  41.3 us
    reduce_scatter x1, waiting for transfers between devices, on_device(): lax.psum_scatter(early_input, 'tensor', scatter_dimension=1, tiled=True)  40.2 us
    all_to_all x1, waiting for transfers between devices, on_device(): lax.all_to_all(value_part, 'expert', split_axis=0, concat_axis=0, tiled=T...  37.6 us
    all_to_all x1, waiting for transfers between devices, on_device(): lax.all_to_all(input_part, 'expert', split_axis=0, concat_axis=0, tiled=T...  33 us
    all_gather x1, blocking collectives, on_device(): lax.all_gather(tokens, 'tensor', axis=1, tiled=True)  31 us
    all_to_all x1, starting transfers between devices, on_device(): lax.all_to_all(x_slots, 'expert', split_axis=0, concat_axis=0, tiled=True)  13.9 us
    all_to_all x1, starting transfers between devices, on_device(): lax.all_to_all(g_slots, 'expert', split_axis=0, concat_axis=0, tiled=True)  7.71 us
  transfers between devices with their start and end apart: 7, of which 5 were waited for; matrix products, arithmetic and copies ran while one was open for 9% of the time, Pallas kernels for 0%

profile of v1, /device:TPU:2, one launch (start us, length us, event | category | flops | bytes accessed | tf_op | source)
XLA Modules:
  0.0 345.6 jit_solution(14536998617973455682)
XLA Ops:
  7.2 1.0 copy.27
  8.2 0.9 stack.2
  9.1 7.1 %all-to-all-start.2 = ((bf16[8,128,256]{1,2,0:T(8,128)(2,1)}), bf16[8,128,256]{1,2,0:T(8,128)(2,1)S(1)}, u32[]{:S(2)}, u32[]{:S(2)}) async-start(bf16[8,128,256]{1,2,0:T(8,128)(2,1)} %stack.2), calls=%async_computation.3 | async-start | bytes 1048576 | tf_op jit(solution)/shard_map/all_to_all | solution.py:47
  16.6 1.8 reduce-window.6
  18.4 0.3 slice_reduce_fusion
  18.7 0.1 fusion.15
  19.2 0.2 fusion.2
  19.4 31.0 %all_gather.3 = bf16[128,2048]{1,0:T(8,128)(2,1)S(1)} all-gather(bf16[128,256]{1,0:T(8,128)(2,1)S(1)} %copy-done.14), channel_id=1, replica_groups=mesh['expert'=64,'tensor'=8] {'tensor'}, dimensions={1}, use_global_device_ids=true | all-gather | bytes 589824 | tf_op jit(solution)/shard_map/all_gather | solution.py:45
  50.4 0.6 convolution_convert_fusion.2
  50.9 1.6 all_to_all.35
  52.6 0.8 copy-done.3
  53.4 13.9 %all-to-all-start = ((bf16[64,6,2048]{2,1,0:T(8,128)(2,1)}), bf16[64,6,2048]{2,1,0:T(8,128)(2,1)S(1)}, u32[]{:S(2)}, u32[]{:S(2)}) async-start(bf16[64,6,2048]{2,1,0:T(8,128)(2,1)} %all_to_all.35), calls=%async_computation | async-start | bytes 4194304 | tf_op jit(solution)/shard_map/all_to_all | solution.py:55
  67.5 0.2 select_reduce_fusion
  67.7 2.8 multiply_convert_fusion
  70.5 3.7 %all_to_all.42 = bf16[64,6,2048]{2,1,0:T(8,128)(2,1)} reshape(bf16[384,2048]{1,0:T(8,128)(2,1)} %multiply_convert_fusion) | data formatting | bytes 3145728 | tf_op jit(solution)/shard_map/all_to_all | solution.py:56
  74.2 42.6 %all-to-all-done = bf16[64,6,2048]{2,1,0:T(8,128)(2,1)S(1)} async-done(((bf16[64,6,2048]{2,1,0:T(8,128)(2,1)}), bf16[64,6,2048]{2,1,0:T(8,128)(2,1)S(1)}, u32[]{:S(2)}, u32[]{:S(2)}) %all-to-all-start) | async-done | bytes 1572896 | tf_op jit(solution)/shard_map/all_to_all | solution.py:55
  116.8 1.3 copy-done.2
  118.1 7.7 %all-to-all-start.3 = ((bf16[64,6,2048]{2,1,0:T(8,128)(2,1)}), bf16[64,6,2048]{2,1,0:T(8,128)(2,1)}, u32[]{:S(2)}, u32[]{:S(2)}) async-start(bf16[64,6,2048]{2,1,0:T(8,128)(2,1)} %all_to_all.42), calls=%async_computation.4 | async-start | bytes 4194304 | tf_op jit(solution)/shard_map/all_to_all | solution.py:56
  125.8 2.6 all_to_all.37
  128.5 1.8 fusion.6
  130.3 0.7 fusion.8
  131.0 0.7 copy-done.9
  131.7 0.6 convolution_convert_fusion
  132.3 1.6 all_to_all.38
  133.9 41.3 %all-to-all-done.3 = bf16[64,6,2048]{2,1,0:T(8,128)(2,1)} async-done(((bf16[64,6,2048]{2,1,0:T(8,128)(2,1)}), bf16[64,6,2048]{2,1,0:T(8,128)(2,1)}, u32[]{:S(2)}, u32[]{:S(2)}) %all-to-all-start.3) | async-done | bytes 1572896 | tf_op jit(solution)/shard_map/all_to_all | solution.py:56
  175.3 7.5 %all-to-all-start.1 = ((bf16[64,6,2048]{2,1,0:T(8,128)(2,1)}), bf16[64,6,2048]{2,1,0:T(8,128)(2,1)S(1)}, u32[]{:S(2)}, u32[]{:S(2)}) async-start(bf16[64,6,2048]{2,1,0:T(8,128)(2,1)} %all_to_all.38), calls=%async_computation.1 | async-start | bytes 4194304 | tf_op jit(solution)/shard_map/all_to_all | solution.py:106
  182.8 3.8 %all_to_all.44 = bf16[384,2048]{1,0:T(8,128)(2,1)} reshape(bf16[64,6,2048]{2,1,0:T(8,128)(2,1)} %all-to-all-done.3) | data formatting | bytes 3145728 | tf_op jit(solution)/shard_map/all_to_all | solution.py:56
  186.6 2.3 fusion.20
  188.9 2.2 convolution_convert_fusion.1
  191.1 3.7 %all_to_all.45 = bf16[64,6,2048]{2,1,0:T(8,128)(2,1)} reshape(bf16[384,2048]{1,0:T(8,128)(2,1)} %convolution_convert_fusion.1) | data formatting | bytes 3145728 | tf_op jit(solution)/shard_map/all_to_all | solution.py:107
  194.8 37.6 %all-to-all-done.1 = bf16[64,6,2048]{2,1,0:T(8,128)(2,1)S(1)} async-done(((bf16[64,6,2048]{2,1,0:T(8,128)(2,1)}), bf16[64,6,2048]{2,1,0:T(8,128)(2,1)S(1)}, u32[]{:S(2)}, u32[]{:S(2)}) %all-to-all-start.1) | async-done | bytes 1572896 | tf_op jit(solution)/shard_map/all_to_all | solution.py:106
  232.4 1.3 copy-done.1
  233.7 7.5 %all-to-all-start.4 = ((bf16[64,6,2048]{2,1,0:T(8,128)(2,1)}), bf16[64,6,2048]{2,1,0:T(8,128)(2,1)S(1)}, u32[]{:S(2)}, u32[]{:S(2)}) async-start(bf16[64,6,2048]{2,1,0:T(8,128)(2,1)} %all_to_all.45), calls=%async_computation.5 | async-start | bytes 4194304 | tf_op jit(solution)/shard_map/all_to_all | solution.py:107
  241.2 0.2 reduce-scatter.3.cloned.1.call-start
  241.4 1.5 fusion.38
  243.0 1.5 fusion.37
  244.5 1.4 fusion.25
  245.9 3.7 %all_to_all.40 = bf16[384,2048]{1,0:T(8,128)(2,1)} reshape(bf16[64,6,2048]{2,1,0:T(8,128)(2,1)} %copy-done.1) | data formatting | bytes 3145728 | tf_op jit(solution)/shard_map/all_to_all | solution.py:106
  249.6 3.9 %convolution_add_fusion.2 = f32[128,2048]{1,0:T(8,128)} fusion(f32[128,2048]{1,0:T(8,128)} %fusion.25, bf16[384,2048]{1,0:T(8,128)(2,1)} %all_to_all.40, f32[384]{0:T(512)S(1)} %select_reduce_fusion, pred[384,128]{1,0:T(8,128)(4,1)S(1)} %fusion.2), kind=kOutput, calls=%fused_computation.6 | convolution fusion | flops 1208369152 | bytes 3720704 | tf_op jit(solution)/shard_map/st,sd->td/dot_general | solution.py:109
  253.6 1.6 fusion.39
  255.1 1.2 fusion.26
  256.4 1.3 convolution_add_fusion.1
  257.7 33.0 %all-to-all-done.4 = bf16[64,6,2048]{2,1,0:T(8,128)(2,1)S(1)} async-done(((bf16[64,6,2048]{2,1,0:T(8,128)(2,1)}), bf16[64,6,2048]{2,1,0:T(8,128)(2,1)S(1)}, u32[]{:S(2)}, u32[]{:S(2)}) %all-to-all-start.4) | async-done | bytes 1572896 | tf_op jit(solution)/shard_map/all_to_all | solution.py:107
  290.7 1.4 all_to_all.47
  292.2 3.2 convolution_add_fusion
  295.4 1.5 convert_element_type.67
  297.0 40.2 %reduce-scatter.5.cloned.1.call-done = f32[128,256]{1,0:T(8,128)} async-done(((f32[128,2048]{1,0:T(8,128)}), f32[128,256]{1,0:T(8,128)}) %reduce-scatter.5.cloned.1.call-update) | async-done | bytes 131088 | tf_op jit(solution)/shard_map/reduce_scatter | solution.py:125
  337.2 1.5 convert_element_type.76
  (48 shorter events, 1.2 us)
Async XLA Ops:
  7.2 124.5 %copy-start = (bf16[1,176,2048]{2,1,0:T(8,128)(2,1)S(1)}, bf16[1,176,2048]{2,1,0:T(8,128)(2,1)}, u32[]{:S(2)}) copy-start(bf16[1,176,2048]{2,1,0:T(8,128)(2,1)} %param.19) | copy-start | bytes 2162692
  7.2 9.0 %copy-start.15 = (s32[128,6]{0,1:T(8,128)S(1)}, s32[128,6]{0,1:T(8,128)}, u32[]{:S(2)}) copy-start(s32[128,6]{0,1:T(8,128)} %param.12) | copy-start | bytes 9220
  8.2 11.1 %copy-start.14 = (bf16[128,256]{1,0:T(8,128)(2,1)S(1)}, bf16[128,256]{1,0:T(8,128)(2,1)}, u32[]{:S(2)}) copy-start(bf16[128,256]{1,0:T(8,128)(2,1)} %param.10) | copy-start | bytes 196612
  9.1 43.5 %all-to-all-start.2 = ((bf16[8,128,256]{1,2,0:T(8,128)(2,1)}), bf16[8,128,256]{1,2,0:T(8,128)(2,1)S(1)}, u32[]{:S(2)}, u32[]{:S(2)}) async-start(bf16[8,128,256]{1,2,0:T(8,128)(2,1)} %stack.2), calls=%async_computation.3 | async-start | bytes 1048576 | tf_op jit(solution)/shard_map/all_to_all | solution.py:47
  52.6 14.7 %copy-start.16 = (f32[128,6]{0,1:T(8,128)S(1)}, f32[128,6]{0,1:T(8,128)}, u32[]{:S(2)}) copy-start(f32[128,6]{0,1:T(8,128)} %param.13) | copy-start | bytes 9220
  52.6 0.8 copy-start.3
  53.4 63.4 %all-to-all-start = ((bf16[64,6,2048]{2,1,0:T(8,128)(2,1)}), bf16[64,6,2048]{2,1,0:T(8,128)(2,1)S(1)}, u32[]{:S(2)}, u32[]{:S(2)}) async-start(bf16[64,6,2048]{2,1,0:T(8,128)(2,1)} %all_to_all.35), calls=%async_computation | async-start | bytes 4194304 | tf_op jit(solution)/shard_map/all_to_all | solution.py:55
  116.8 1.3 copy-start.2
  118.1 57.2 %all-to-all-start.3 = ((bf16[64,6,2048]{2,1,0:T(8,128)(2,1)}), bf16[64,6,2048]{2,1,0:T(8,128)(2,1)}, u32[]{:S(2)}, u32[]{:S(2)}) async-start(bf16[64,6,2048]{2,1,0:T(8,128)(2,1)} %all_to_all.42), calls=%async_computation.4 | async-start | bytes 4194304 | tf_op jit(solution)/shard_map/all_to_all | solution.py:56
  128.4 1.9 copy-start.12
  130.3 2.0 copy-start.8
  131.0 0.7 copy-start.9
  175.3 57.1 %all-to-all-start.1 = ((bf16[64,6,2048]{2,1,0:T(8,128)(2,1)}), bf16[64,6,2048]{2,1,0:T(8,128)(2,1)S(1)}, u32[]{:S(2)}, u32[]{:S(2)}) async-start(bf16[64,6,2048]{2,1,0:T(8,128)(2,1)} %all_to_all.38), calls=%async_computation.1 | async-start | bytes 4194304 | tf_op jit(solution)/shard_map/all_to_all | solution.py:106
  186.6 2.3 copy-start.11
  186.6 2.3 copy-start.13
  232.3 1.3 copy-start.1
  233.7 57.1 %all-to-all-start.4 = ((bf16[64,6,2048]{2,1,0:T(8,128)(2,1)}), bf16[64,6,2048]{2,1,0:T(8,128)(2,1)S(1)}, u32[]{:S(2)}, u32[]{:S(2)}) async-start(bf16[64,6,2048]{2,1,0:T(8,128)(2,1)} %all_to_all.45), calls=%async_computation.5 | async-start | bytes 4194304 | tf_op jit(solution)/shard_map/all_to_all | solution.py:107
  241.2 54.2 %reduce-scatter.3.cloned.1.call-start = ((), (), s32[]{:S(2)}) async-start(), calls=%async_computation.7 | async-start | bytes 1179648 | tf_op jit(solution)/shard_map/reduce_scatter | solution.py:124
  241.4 3.1 copy-start.5
  243.0 1.5 copy-start.10
  249.6 3.9 %copy-start.4 = (bf16[8,128,256]{1,2,0:T(8,128)(2,1)S(1)}, bf16[8,128,256]{1,2,0:T(8,128)(2,1)}, u32[]{:S(2)}) copy-start(bf16[8,128,256]{1,2,0:T(8,128)(2,1)} %copy-done.3) | copy-start | bytes 1572868
  253.5 83.7 %reduce-scatter.5.cloned.1.call-start = ((), (), s32[]{:S(2)}) async-start(), calls=%async_computation.8 | async-start | bytes 1179648 | tf_op jit(solution)/shard_map/reduce_scatter | solution.py:125
  253.6 1.6 copy-start.6
  253.6 2.8 copy-start.7
Sparse Core Ops, SparseCore 0:
  253.6 40.5 reduce-scatter.2
  297.0 40.1 reduce-scatter.4
